TPU v7x, 256 devices: a whole 4x4x8 slice. The times are simulated.
256 devices in a mesh: region: 64 (over x, z, core), obs: 4 (over y).
Axes of the slice: x: 4, y: 4, z: 8, core: 2. Of those that a mesh axis runs over, the one named last changes fastest.
Arguments:
- state_pert: bfloat16 [8192, 128, 512], P('region', None, 'obs'), may hold values from -6 to 6
- state_mean: float32 [8192, 512], P('region', 'obs'), may hold values from -6 to 6
- obs_pert: bfloat16 [8192, 128, 128], P(('region', 'obs')), may hold values from -6 to 6
- innov: float32 [8192, 128], P(('region', 'obs')), may hold values from -6 to 6
- obs_weight: float32 [8192, 128], P(('region', 'obs')), may hold values from 0.1 to 1
- block_type: int32 [8192], P(('region', 'obs')), may hold values from 0 to 7, as said below
- type_prec: float32 [8], replicated, may hold values from 0.3 to 3
- block_list: int32 [8192, 8], P('region', 'obs'), may hold values from 0 to 31
- block_count: int32 [8192, 4], P('region', 'obs'), may hold values from 1 to 2
- obs_clusters: int32 [64], replicated, may hold values from 1 to 128, 2048 in all
Outputs:
- analysis: bfloat16 [8192, 128, 512], P('region', None, 'obs')
Inputs may be any that keep to these rules, and one draw needn't show every extreme that they name: `block_type`: blocks held on index o of obs have types o * 2 to (o + 1) * 2 - 1. `block_list`: entries name blocks of the pool of the cluster's own tile and the entry's index of obs. `obs_clusters`: the counts sum to 2048.
All inputs are finite; a program needn't handle non-finite values.
Results may differ from a plain program's by a relative error of at most 0.0021.
Values may be sent and summed in bfloat16 or wider, within the bound.
A program may use at most 128 MiB of HBM per device.

v0:
```python
import jax
import jax.numpy as jnp
from jax import lax
from jax.sharding import PartitionSpec as P

ITERS = 12
PER_OWNER = 32


def product(left, right):
    return jnp.einsum("cij,cjk->cik", left, right, precision=lax.Precision.HIGHEST)


def transform(gram_sums, projected, members):
    identity = jnp.eye(members, dtype=jnp.float32)
    matrix = identity + gram_sums / (members - 1.0)
    norm_sum = jnp.sqrt(jnp.sum(matrix * matrix, axis=(1, 2)))
    iterate_y = matrix / norm_sum[:, None, None]
    iterate_z = jnp.broadcast_to(identity, matrix.shape)

    def newton_step(turn, state_pair):
        current_y, current_z = state_pair
        turn_matrix = 1.5 * identity - 0.5 * product(current_z, current_y)
        return (product(current_y, turn_matrix), product(turn_matrix, current_z))

    iterate_y, iterate_z = lax.fori_loop(0, ITERS, newton_step, (iterate_y, iterate_z))
    inverse = product(iterate_z, iterate_z) / norm_sum[:, None, None]
    mean_weights = jnp.einsum("ckl,cl->ck", inverse, projected, precision=lax.Precision.HIGHEST) / (
        members - 1.0
    )
    sqrt_inverse = iterate_z / jnp.sqrt(norm_sum)[:, None, None]
    return (sqrt_inverse + mean_weights[:, :, None]).astype(jnp.bfloat16)


def partials(cluster_pert, cluster_weights, cluster_innov):
    scaled = (
        cluster_pert.astype(jnp.float32) * cluster_weights.astype(jnp.float32)[:, :, None, :]
    ).astype(jnp.bfloat16)
    gram_sums = jnp.einsum(
        "cbko,cblo->ckl", cluster_pert, scaled, preferred_element_type=jnp.float32
    )
    projected = jnp.einsum(
        "cbko,cbo->ck", cluster_pert, cluster_innov, preferred_element_type=jnp.float32
    )
    return (gram_sums, projected)


def local(
    state_pert,
    state_mean,
    obs_pert,
    innov,
    obs_weight,
    block_type,
    type_prec,
    block_list,
    block_count,
    obs_clusters,
):
    members = obs_pert.shape[1]
    clusters = block_list.shape[0]
    type_total = type_prec.shape[0]
    type_match = (block_type[:, None] == jnp.arange(type_total, dtype=jnp.int32)[None, :]).astype(
        jnp.float32
    )
    precision_row = jnp.sum(type_match * type_prec[None, :], axis=1)
    weighted = obs_weight * precision_row[:, None]
    weight_rows = weighted.astype(jnp.bfloat16)
    weighted_innov = (weighted * innov).astype(jnp.bfloat16)
    live_mask = jnp.arange(block_list.shape[1], dtype=jnp.int32)[None, :] < block_count
    zero_value = jnp.zeros((), jnp.bfloat16)
    cluster_pert = obs_pert[block_list]
    cluster_weights = jnp.where(live_mask[:, :, None], weight_rows[block_list], zero_value)
    cluster_innov = jnp.where(live_mask[:, :, None], weighted_innov[block_list], zero_value)
    gram_sums, projected = partials(cluster_pert, cluster_weights, cluster_innov)
    region_size = lax.axis_size("region")
    here = lax.axis_index("region")
    starts = jnp.cumsum(obs_clusters) - obs_clusters
    local_index = jnp.arange(clusters, dtype=jnp.int32)
    observed = local_index < obs_clusters[here]
    identity = jnp.eye(members, dtype=jnp.bfloat16)
    capacity = (clusters + region_size - 1) // region_size
    slot_total = region_size * capacity
    global_order = starts[here] + local_index
    owner = global_order % region_size
    slot_index = owner * capacity + local_index // region_size
    slot_index = jnp.where(observed, slot_index, slot_total)

    def into_slots(values):
        return (
            jnp.zeros((slot_total,) + values.shape[1:], values.dtype)
            .at[slot_index]
            .set(values, mode="drop")
        )

    received = (
        lax.all_to_all(into_slots(gram_sums), "region", split_axis=0, concat_axis=0, tiled=True),
        lax.all_to_all(into_slots(projected), "region", split_axis=0, concat_axis=0, tiled=True),
    )
    slot_ids = jnp.arange(slot_total, dtype=jnp.int32)
    sender = slot_ids // capacity
    sender_start = starts[sender]
    sender_local = jnp.mod(here - sender_start, region_size) + slot_ids % capacity * region_size
    slot_live = sender_local < obs_clusters[sender]
    row_index = jnp.where(slot_live, (sender_start + sender_local) // region_size, PER_OWNER)
    compact_gram = (
        jnp.zeros((PER_OWNER, members, members), jnp.float32)
        .at[row_index]
        .set(received[0], mode="drop")
    )
    compact_proj = (
        jnp.zeros((PER_OWNER, members), jnp.float32).at[row_index].set(received[1], mode="drop")
    )
    owned_gram, owned_proj = (
        lax.psum_scatter(compact_gram, "obs", scatter_dimension=0, tiled=True),
        lax.psum_scatter(compact_proj, "obs", scatter_dimension=0, tiled=True),
    )
    my_transforms = transform(owned_gram, owned_proj, members)
    all_transforms = lax.all_gather(my_transforms, "obs", axis=0, tiled=True)
    picked = all_transforms[jnp.minimum(row_index, PER_OWNER - 1)]
    back = jnp.where(slot_live[:, None, None], picked, zero_value)
    returned = lax.all_to_all(back, "region", split_axis=0, concat_axis=0, tiled=True)
    fetched = returned[jnp.minimum(slot_index, slot_total - 1)]
    transform_rows = jnp.where(observed[:, None, None], fetched, identity[None])
    mixed = jnp.einsum(
        "cij,cip->cjp", transform_rows, state_pert, preferred_element_type=jnp.float32
    )
    return (state_mean[:, None, :] + mixed).astype(jnp.bfloat16)


def solution(mesh):
    placed = (
        P("region", None, "obs"),
        P("region", "obs"),
        P(("region", "obs"), None, None),
        P(("region", "obs"), None),
        P(("region", "obs"), None),
        P(("region", "obs")),
        P(),
        P("region", "obs"),
        P("region", "obs"),
        P(),
    )
    return jax.shard_map(
        local, mesh=mesh, in_specs=placed, out_specs=P("region", None, "obs"), check_vma=False
    )
```

profile of v0, /device:TPU:1, one launch (start us, length us, event | category | flops | bytes accessed | tf_op | source)
XLA Modules:
  0.0 513.6 jit_solution(8140624896217482601)
XLA Ops:
  8.1 1.2 dynamic_slice.6
  15.0 8.6 %gather_fusion.2 = bf16[256,128,128]{2,1,0:T(8,128)(2,1)} fusion(bf16[32,128,128]{2,1,0:T(8,128)(2,1)S(1)} %copy-done, s32[1024]{0:T(1024)S(1)} %pad_clamp_fusion.2), kind=kCustom, calls=%fused_computation.2 | custom fusion | bytes 16778240 | tf_op jit(solution)/shard_map/gather | solution.py:72
  23.6 1.2 fusion.36
  25.1 11.4 %fusion.9 = f32[128,128,128]{2,1,0:T(8,128)} fusion(bf16[128,2,128,128]{3,2,1,0:T(8,128)(2,1)} %bitcast.80, f32[128,2,128]{2,1,0:T(2,128)S(1)} %get-tuple-element.59), kind=kOutput, calls=%fused_computation.25 | convolution fusion | flops 1086324736 | bytes 16908288 | tf_op jit(solution)/shard_map/cbko,cblo->ckl/dot_general | solution.py:39
  36.4 4.3 broadcast_in_dim.99
  40.7 23.5 %scatter_fusion = f32[128,128,128]{2,1,0:T(8,128)} fusion(f32[128,128,128]{2,1,0:T(8,128)} %broadcast_in_dim.99, s32[128]{0:T(128)S(1)} %fusion.36, f32[128,128,128]{2,1,0:T(8,128)} %fusion.9), kind=kCustom, calls=%fused_computation.7 | custom fusion | bytes 25166336 | tf_op jit(solution)/shard_map/scatter | solution.py:93
  64.2 11.0 %all-to-all-start = ((f32[128,128,128]{2,1,0:T(8,128)}), f32[128,128,128]{2,1,0:T(8,128)}, u32[]{:S(2)}, u32[]{:S(2)}) async-start(f32[128,128,128]{2,1,0:T(8,128)} %scatter_fusion), calls=%async_computation | async-start | bytes 16777216 | tf_op jit(solution)/shard_map/all_to_all | solution.py:97
  75.2 1.2 gather_fusion.1
  76.5 1.2 gather_fusion
  77.7 183.2 %all-to-all-done = f32[128,128,128]{2,1,0:T(8,128)} async-done(((f32[128,128,128]{2,1,0:T(8,128)}), f32[128,128,128]{2,1,0:T(8,128)}, u32[]{:S(2)}, u32[]{:S(2)}) %all-to-all-start) | async-done | bytes 8388640 | tf_op jit(solution)/shard_map/all_to_all | solution.py:97
  261.2 14.4 %scatter_fusion.1 = f32[32,128,128]{2,1,0:T(8,128)S(1)} fusion(f32[32,128,128]{2,1,0:T(8,128)S(1)} %broadcast_in_dim.64, s32[128]{0:T(128)S(1)} %fusion.35, f32[128,128,128]{2,1,0:T(8,128)} %all-to-all-done), kind=kCustom, calls=%fused_computation.8 | custom fusion | bytes 25166336 | tf_op jit(solution)/shard_map/scatter | solution.py:109
  275.5 1.3 copy-done.3
  276.9 5.6 %fusion.14 = f32[128,1,128,1]{2,1,3,0:T(1,128)S(1)} fusion(bf16[128,2,128,128]{3,2,1,0:T(8,128)(2,1)} %bitcast.81, bf16[128,2,128,1]{2,1,0,3:T(2,128)(2,1)S(1)} %get-tuple-element.58), kind=kOutput, calls=%fused_computation.32 | convolution fusion | flops 8388608 | bytes 8519680 | tf_op jit(solution)/shard_map/cbko,cbo->ck/dot_general | solution.py:42
  282.5 1.5 scatter_custom_fusion.2
  284.0 5.9 %all-to-all-start.1 = ((f32[64,2,128]{2,1,0:T(2,128)}), f32[64,2,128]{2,1,0:T(2,128)S(1)}, u32[]{:S(2)}, u32[]{:S(2)}) async-start(f32[64,2,128]{2,1,0:T(2,128)} %bitcast.17), calls=%async_computation.2 | async-start | bytes 131072 | tf_op jit(solution)/shard_map/all_to_all | solution.py:98
  291.2 8.5 %all-to-all-done.1 = f32[64,2,128]{2,1,0:T(2,128)S(1)} async-done(((f32[64,2,128]{2,1,0:T(2,128)}), f32[64,2,128]{2,1,0:T(2,128)S(1)}, u32[]{:S(2)}, u32[]{:S(2)}) %all-to-all-start.1) | async-done | bytes 65568 | tf_op jit(solution)/shard_map/all_to_all | solution.py:98
  300.5 13.4 %all-reduce = f32[32,128]{1,0:T(8,128)S(1)} all-reduce(f32[32,128]{1,0:T(8,128)S(1)} %scatter_custom_fusion.3), channel_id=3, replica_groups=mesh['region'=64,'obs'=4] {'obs'}, use_global_device_ids=true, to_apply=%region_10.11.clone | all-reduce | flops 4096 | bytes 32768
  313.9 1.2 multiply_reduce_fusion
  315.2 1.2 fusion.13
  316.6 36.0 %while.13 = (s32[]{:T(128)}, f32[8,128,128]{1,2,0:T(8,128)S(1)}, f32[8,128,128]{2,1,0:T(8,128)S(1)}, s32[]{:T(128)}) while((s32[]{:T(128)}, f32[8,128,128]{1,2,0:T(8,128)S(1)}, f32[8,128,128]{2,1,0:T(8,128)S(1)}, s32[]{:T(128)}) %tuple.29), condition=%wide.region_7.8_spmd.clone, body=%wide.region_6.7_spmd.clone.sunk | while | flops 604274688 | bytes 6946869 | solution.py:26
  316.7 1.2 fusion.70
  319.7 1.2 fusion.70
  322.7 1.2 fusion.70
  324.6 1.0 convolution_bitcast_fusion.2
  325.7 1.2 fusion.70
  327.6 1.0 convolution_bitcast_fusion.2
  328.7 1.2 fusion.70
  330.6 1.0 convolution_bitcast_fusion.2
  331.7 1.2 fusion.70
  333.6 1.0 convolution_bitcast_fusion.2
  334.7 1.2 fusion.70
  336.6 1.0 convolution_bitcast_fusion.2
  337.7 1.2 fusion.70
  339.6 1.0 convolution_bitcast_fusion.2
  340.7 1.2 fusion.70
  343.7 1.2 fusion.70
  345.6 1.0 convolution_bitcast_fusion.2
  346.7 1.2 fusion.70
  348.6 1.0 convolution_bitcast_fusion.2
  349.7 1.2 fusion.70
  355.2 22.3 %all-gather.2.cloned.1.call-done = bf16[32,128,128]{2,1,0:T(8,128)(2,1)} async-done(((bf16[8,128,128]{2,1,0:T(8,128)(2,1)}), bf16[32,128,128]{2,1,0:T(8,128)(2,1)}) %all-gather.2.cloned.1.call-update) | async-done | bytes 1048592 | tf_op jit(solution)/shard_map/all_gather | solution.py:119
  377.5 4.3 gather_fusion.5
  381.8 4.6 broadcast_select_fusion
  386.4 11.9 %all-to-all-start.2 = ((bf16[128,128,128]{2,1,0:T(8,128)(2,1)}), bf16[128,128,128]{2,1,0:T(8,128)(2,1)}, u32[]{:S(2)}, u32[]{:S(2)}) async-start(bf16[128,128,128]{2,1,0:T(8,128)(2,1)} %broadcast_select_fusion), calls=%async_computation.3 | async-start | bytes 8388608 | tf_op jit(solution)/shard_map/all_to_all | solution.py:122
  398.8 1.2 fusion.38
  400.1 94.1 %all-to-all-done.2 = bf16[128,128,128]{2,1,0:T(8,128)(2,1)} async-done(((bf16[128,128,128]{2,1,0:T(8,128)(2,1)}), bf16[128,128,128]{2,1,0:T(8,128)(2,1)}, u32[]{:S(2)}, u32[]{:S(2)}) %all-to-all-start.2) | async-done | bytes 4194336 | tf_op jit(solution)/shard_map/all_to_all | solution.py:122
  494.1 5.3 %gather_fusion.6 = bf16[128,128,128]{2,1,0:T(8,128)(2,1)} fusion(bf16[128,128,128]{2,1,0:T(8,128)(2,1)} %all-to-all-done.2, s32[1024]{0:T(1024)S(1)} %pad_clamp_fusion), kind=kCustom, calls=%fused_computation.6 | custom fusion | bytes 8389120 | tf_op jit(solution)/shard_map/gather | solution.py:123
  499.5 7.3 %add_convert_fusion = bf16[128,128,128]{2,1,0:T(8,128)(2,1)} fusion(f32[128,128]{1,0:T(8,128)S(1)} %copy-done.4, bf16[128,128,128]{2,1,0:T(8,128)(2,1)} %param.12, bf16[128,128,128]{2,1,0:T(8,128)(2,1)} %gather_fusion.6, pred[128]{0:T(512)(128)(4,1)S(1)} %iota_compare_fusion.4, bf16[128,128]{1,0:T(8,128)(2,1)S(1)} %fusion.18), kind=kOutput, calls=%fused_computation.19 | convolution fusion | flops 543162368 | bytes 12681344 | tf_op jit(solution)/shard_map/cij,cip->cjp/dot_general | solution.py:125
  (104 shorter events, 25.5 us)
Async XLA Ops:
  6.5 8.5 %copy-start = (bf16[32,128,128]{2,1,0:T(8,128)(2,1)S(1)}, bf16[32,128,128]{2,1,0:T(8,128)(2,1)}, u32[]{:S(2)}) copy-start(bf16[32,128,128]{2,1,0:T(8,128)(2,1)} %param.14) | copy-start | bytes 3145732
  64.2 11.1 %copy-start.2 = (s32[64]{0:T(128)S(1)}, s32[64]{0:T(128)}, u32[]{:S(2)}) copy-start(s32[64]{0:T(128)} %param.21) | copy-start | bytes 772
  64.2 196.7 %all-to-all-start = ((f32[128,128,128]{2,1,0:T(8,128)}), f32[128,128,128]{2,1,0:T(8,128)}, u32[]{:S(2)}, u32[]{:S(2)}) async-start(f32[128,128,128]{2,1,0:T(8,128)} %scatter_fusion), calls=%async_computation | async-start | bytes 16777216 | tf_op jit(solution)/shard_map/all_to_all | solution.py:97
  75.2 238.8 %reduce-scatter.2.cloned.1.call-start = ((), (), s32[]{:S(2)}) async-start(), calls=%async_computation.4 | async-start | bytes 2621440 | tf_op jit(solution)/shard_map/reduce_scatter | solution.py:115
  275.5 1.3 copy-start.3
  275.5 14.4 %copy-start.5 = (u32[256]{0:T(256)S(1)}, u32[256]{0:T(256)}, u32[]{:S(2)}) copy-start(u32[256]{0:T(256)} %constant.126) | copy-start | bytes 3076
  284.0 15.7 %all-to-all-start.1 = ((f32[64,2,128]{2,1,0:T(2,128)}), f32[64,2,128]{2,1,0:T(2,128)S(1)}, u32[]{:S(2)}, u32[]{:S(2)}) async-start(f32[64,2,128]{2,1,0:T(2,128)} %bitcast.17), calls=%async_computation.2 | async-start | bytes 131072 | tf_op jit(solution)/shard_map/all_to_all | solution.py:98
  289.9 87.6 %all-gather.2.cloned.1.call-start = ((), (), s32[]{:S(2)}) async-start(), calls=%async_computation.5 | async-start | bytes 1310720 | tf_op jit(solution)/shard_map/all_gather | solution.py:119
  386.4 113.1 %copy-start.4 = (f32[128,128]{1,0:T(8,128)S(1)}, f32[128,128]{1,0:T(8,128)}, u32[]{:S(2)}) copy-start(f32[128,128]{1,0:T(8,128)} %param.13) | copy-start | bytes 196612
  386.4 107.8 %all-to-all-start.2 = ((bf16[128,128,128]{2,1,0:T(8,128)(2,1)}), bf16[128,128,128]{2,1,0:T(8,128)(2,1)}, u32[]{:S(2)}, u32[]{:S(2)}) async-start(bf16[128,128,128]{2,1,0:T(8,128)(2,1)} %broadcast_select_fusion), calls=%async_computation.3 | async-start | bytes 8388608 | tf_op jit(solution)/shard_map/all_to_all | solution.py:122
  494.1 12.7 %copy-start.1 = (bf16[32,128,128]{2,1,0:T(8,128)(2,1)S(1)}, bf16[32,128,128]{2,1,0:T(8,128)(2,1)}, u32[]{:S(2)}) copy-start(bf16[32,128,128]{2,1,0:T(8,128)(2,1)} %param.14) | copy-start | bytes 3145732
Sparse Core Ops, SparseCore 0:
  277.0 29.0 reduce-scatter.1
  355.2 22.1 all-gather.1
where the time goes:
time: 515 us; the launch traced here: 514 us
  waiting for transfers between devices  308 us (60%)
  local copies, waits for them, and re-layouts  72.9 us (14%)
  matrix products  60.2 us (12%)
  starting transfers between devices  28.8 us (6%)
  other arithmetic  15.2 us (3%)
  between operations  14.3 us (3%)
  blocking collectives  13.4 us (3%)
    all_to_all x1, waiting for transfers between devices, local(): lax.all_to_all(into_slots(gram_sums), 'region', split_axis=0, concat_axis...  183 us
    all_to_all x1, waiting for transfers between devices, local(): lax.all_to_all(back, 'region', split_axis=0, concat_axis=0, tiled=True)  94.1 us
    dot_general x37, matrix products, product(): jnp.einsum('cij,cjk->cik', left, right, precision=lax.Precision.HIGHEST)  35 us
    scatter x2, local copies, waits for them, and re-layouts, into_slots(): return jnp.zeros((slot_total,) + values.shape[1:], values.dtype).at[slot_...  25 us
    all_gather x1, waiting for transfers between devices, local(): all_transforms = lax.all_gather(my_transforms, 'obs', axis=0, tiled=True)  22.3 us
    scatter x1, local copies, waits for them, and re-layouts, local(): compact_gram = jnp.zeros((PER_OWNER, members, members), jnp.float32).at[r...  14.4 us
    unnamed x1, blocking collectives  13.4 us
    all_to_all x1, starting transfers between devices, local(): lax.all_to_all(back, 'region', split_axis=0, concat_axis=0, tiled=True)  11.9 us
  transfers between devices with their start and end apart: 5, of which 4 were waited for; matrix products, arithmetic and copies ran while one was open for 3% of the time, Pallas kernels for 0%

commit v1 on v0

v1 whole, which is shorter than its diff:
```python
import functools

import jax
import jax.numpy as jnp
from jax import lax
from jax.experimental import pallas as pl
from jax.experimental.pallas import tpu as pltpu
from jax.sharding import PartitionSpec as P

MESH = pl.DeviceIdType.MESH
BF = jnp.bfloat16
F32 = jnp.float32
OBS = 4
POOL = 32
SLOTS = POOL + 1
CHUNKS = 8
PER = POOL // CHUNKS
GROUP = 8
OWN = 32
GROUPS = OWN // GROUP
HALF = GROUP // 2
COEF = (2.25, -2.4375, 1.6875, -0.5625, 0.0625)


def split(a):
    high = a.astype(BF)
    return high, (a - high.astype(F32)).astype(BF)


def product(left, right):
    left_high, left_low = left
    right_high, right_low = right
    row = jnp.concatenate([right_high, right_low], axis=1)
    both = jnp.dot(
        jnp.concatenate([left_high, left_low], axis=1),
        jnp.concatenate([row, row], axis=0),
        preferred_element_type=F32,
    )
    k = both.shape[1] // 2
    return both[:, :k] + both[:, k:]


def inverse_root(matrices, eye):
    every = range(len(matrices))
    w = list(matrices)
    w_parts = [split(a) for a in w]
    y, z = w_parts, None
    for step in range(6):
        if step:
            w = [product(z[i], y[i]) for i in every]
            w_parts = [split(a) for a in w]
        w2 = [product(a, a) for a in w_parts]
        tail = [split(COEF[3] * w[i] + COEF[4] * w2[i]) for i in every]
        w2_parts = [split(a) for a in w2]
        turn = [
            (COEF[0] * eye + COEF[1] * w[i]) + (COEF[2] * w2[i] + product(w2_parts[i], tail[i]))
            for i in every
        ]
        turn_parts = [split(a) for a in turn]
        if step < 5:
            y = [split(product(y[i], turn_parts[i])) for i in every]
        if step:
            z_full = [product(turn_parts[i], z[i]) for i in every]
            z = [split(a) for a in z_full]
        else:
            z = turn_parts
    return z_full, z


def solve_kernel(
    lists_ref, type_ref, prec_ref, weight_ref, innov_ref, pool_ref, out_ref,
    pool, rows, lists, index, gram, proj, mine,
    local_sem, small_send, small_recv, send, recv, pass_send, pass_recv,
    t_local, t_send, t_recv, tp_send, tp_recv,
):
    me = lax.axis_index("obs")
    right, left, far = lax.rem(me + 1, OBS), lax.rem(me + 3, OBS), lax.rem(me + 2, OBS)

    def remote(src, dst, send_sem, recv_sem, to):
        return pltpu.make_async_remote_copy(
            src_ref=src, dst_ref=dst, send_sem=send_sem, recv_sem=recv_sem,
            device_id={"obs": to}, device_id_type=MESH,
        )

    barrier = pltpu.get_barrier_semaphore()
    for other in (right, left, far):
        pl.semaphore_signal(barrier, inc=1, device_id={"obs": other}, device_id_type=MESH)

    keep = pltpu.make_async_copy(pool_ref, pool.at[me], local_sem)
    keep.start()
    for b in range(POOL):
        weighted = weight_ref[pl.ds(b, 1), :] * prec_ref[type_ref[b]]
        rows[me, pl.ds(b, 1), :] = weighted.astype(BF).astype(F32)
        rows[me, pl.ds(POOL + b, 1), :] = (weighted * innov_ref[pl.ds(b, 1), :]).astype(BF).astype(F32)
    lists[me] = lists_ref[...]
    eye = (
        lax.broadcasted_iota(jnp.int32, (128, 128), 0) == lax.broadcasted_iota(jnp.int32, (128, 128), 1)
    ).astype(F32)
    for o in range(OBS):
        gram[o * SLOTS + POOL] = jnp.zeros((128, 128), F32)
        proj[o, pl.ds(POOL, 8), :] = jnp.zeros((8, 128), F32)
    pl.semaphore_wait(barrier, 3)

    small = []
    for d, to in enumerate((right, left, far)):
        for j, ref in enumerate((rows, lists)):
            small.append(remote(ref.at[me], ref.at[me], small_send.at[d, j], small_recv.at[d, j], to))
            small[-1].start()

    def piece(o, k):
        return pool.at[o, pl.ds(k * PER, PER)]

    sends = []
    for k in range(CHUNKS):
        for d, to in enumerate((right, left)):
            sends.append(
                remote(pool_ref.at[pl.ds(k * PER, PER)], piece(me, k), send.at[d, k], recv.at[d, k], to)
            )
            sends[-1].start()

    def block_grams(o, k):
        for j in range(PER):
            b = k * PER + j
            pert = pool[o, b]
            weight = rows[o, pl.ds(b, 1), :]
            innov = rows[o, pl.ds(POOL + b, 1), :]
            scaled = (pert.astype(F32) * weight).astype(BF)
            lhs = jnp.concatenate([scaled, jnp.broadcast_to(innov, (16, 128)).astype(BF)], axis=0)
            res = lax.dot_general(lhs, pert, (((1,), (1,)), ((), ())), preferred_element_type=F32)
            gram[o * SLOTS + b] = res[:128]
            proj[o, pl.ds(b, 1), :] = res[128:129]

    keep.wait()

    def own_step(k, _):
        block_grams(me, k)
        return 0

    lax.fori_loop(0, CHUNKS, own_step, 0)
    for c in small:
        c.wait_recv()
    to_index = pltpu.make_async_copy(lists, index, local_sem)
    to_index.start()
    passes = []
    for k in range(CHUNKS):
        for d, source, to in ((0, left, right), (1, right, left)):
            remote(piece(source, k), piece(source, k), send.at[d, k], recv.at[d, k], to).wait_recv()
            if k % 2 == d:
                passes.append(
                    remote(piece(source, k), piece(source, k), pass_send.at[k], pass_recv.at[k], to)
                )
                passes[-1].start()
        block_grams(left, k)
        block_grams(right, k)
    to_index.wait()
    for k in range(CHUNKS):
        passes[k].wait_recv()
        block_grams(far, k)

    def t_piece(o, g, at, size):
        return out_ref.at[pl.ds(o * OWN + g * GROUP + at, size)]

    def t_first(g, d, to):
        return remote(
            mine.at[pl.ds(g * GROUP, GROUP)], t_piece(me, g, 0, GROUP), t_send.at[d, g], t_recv.at[d, g], to
        )

    def t_pass(g, d, source, to):
        return remote(
            t_piece(source, g, d * HALF, HALF), t_piece(source, g, d * HALF, HALF),
            tp_send.at[d, g], tp_recv.at[d, g], to,
        )

    def forward(g):
        for d, source, to in ((0, left, right), (1, right, left)):
            t_first(g, d, to).wait_recv()
            t_pass(g, d, source, to).start()

    def solve_group(g, _):
        matrices, norms, vectors = [], [], []
        for i in range(GROUP):
            c = me * OWN + g * GROUP + i
            total, vector = None, None
            for o in range(OBS):
                for m in range(2):
                    b = index[o, m, c]
                    one, row = gram[o * SLOTS + b], proj[o, pl.ds(b, 1), :]
                    total = one if total is None else total + one
                    vector = row if vector is None else vector + row
            matrix = eye + total * (1.0 / 127.0)
            square = jnp.sum(jnp.sum(matrix * matrix, axis=0, keepdims=True), axis=1, keepdims=True)
            scale = lax.rsqrt(square)
            matrices.append(matrix * scale)
            norms.append(scale)
            vectors.append(vector)
        full, parts = inverse_root(matrices, eye)
        for i in range(GROUP):
            row = jnp.broadcast_to(vectors[i] * (norms[i] * (1.0 / 127.0)), (16, 128))
            row = product(split(row), parts[i])
            row = product(split(row), parts[i])
            solved = full[i] * jnp.sqrt(norms[i]) + row[0:1]
            mine[g * GROUP + i] = solved.astype(BF)
        for d, to in ((0, right), (1, left)):
            t_first(g, d, to).start()
        pltpu.make_async_copy(
            mine.at[pl.ds(g * GROUP, GROUP)], t_piece(me, g, 0, GROUP), t_local.at[g]
        ).start()

        @pl.when(g > 0)
        def _():
            forward(g - 1)

        return 0

    lax.fori_loop(0, GROUPS, solve_group, 0)
    forward(GROUPS - 1)
    for g in range(GROUPS):
        for d, to in ((0, right), (1, left)):
            t_pass(g, d, far, to).wait_recv()
            t_pass(g, d, far, to).wait_send()
            t_first(g, d, to).wait_send()
        pltpu.make_async_copy(
            mine.at[pl.ds(g * GROUP, GROUP)], t_piece(me, g, 0, GROUP), t_local.at[g]
        ).wait()
    for c in small + sends + passes:
        c.wait_send()


APPLY = 8


def apply_kernel(count_ref, t_ref, x_ref, mean_ref, out_ref):
    count = count_ref[lax.axis_index("region")]
    step = pl.program_id(0)
    for i in range(APPLY):
        x = x_ref[i]
        mixed = jnp.dot(t_ref[i], x, preferred_element_type=F32)
        mixed = jnp.where(step * APPLY + i < count, mixed, x.astype(F32))
        out_ref[i] = (mixed + mean_ref[pl.ds(i, 1), :]).astype(BF)


def local(
    state_pert, state_mean, obs_pert, innov, obs_weight, block_type, type_prec, block_list, block_count, obs_clusters
):
    clusters, members, points = state_pert.shape
    live = jnp.arange(block_list.shape[1], dtype=jnp.int32)[None, :] < block_count
    lists = jnp.where(live, block_list, POOL).T
    lists = jnp.pad(lists, ((0, 8 - lists.shape[0]), (0, 0)))
    dma, regular = pltpu.SemaphoreType.DMA, pltpu.SemaphoreType.REGULAR
    vmem, smem = pl.BlockSpec(memory_space=pltpu.VMEM), pl.BlockSpec(memory_space=pltpu.SMEM)
    anywhere = pl.BlockSpec(memory_space=pl.ANY)
    transforms = pl.pallas_call(
        solve_kernel,
        out_shape=jax.ShapeDtypeStruct((clusters, members, members), BF),
        in_specs=[vmem, smem, smem, vmem, vmem, anywhere],
        out_specs=anywhere,
        scratch_shapes=[
            pltpu.VMEM((OBS, POOL, members, 128), BF),
            pltpu.VMEM((OBS, 2 * POOL, 128), F32),
            pltpu.VMEM((OBS, 8, clusters), jnp.int32),
            pltpu.SMEM((OBS, 8, clusters), jnp.int32),
            pltpu.VMEM((OBS * SLOTS, members, members), F32),
            pltpu.VMEM((OBS, POOL + 8, members), F32),
            pltpu.VMEM((OWN, members, members), BF),
            dma,
            dma((3, 2)), dma((3, 2)),
            dma((2, CHUNKS)), dma((2, CHUNKS)),
            dma((CHUNKS,)), dma((CHUNKS,)),
            dma((GROUPS,)),
            dma((2, GROUPS)), dma((2, GROUPS)),
            dma((2, GROUPS)), dma((2, GROUPS)),
        ],
        compiler_params=pltpu.CompilerParams(
            collective_id=0, has_side_effects=True, vmem_limit_bytes=40 << 20
        ),
        name="solve",
    )(lists, block_type, type_prec, obs_weight, innov, obs_pert)
    return pl.pallas_call(
        apply_kernel,
        grid=(clusters // APPLY,),
        out_shape=jax.ShapeDtypeStruct(state_pert.shape, BF),
        in_specs=[
            smem,
            pl.BlockSpec((APPLY, members, members), lambda s: (s, 0, 0)),
            pl.BlockSpec((APPLY, members, points), lambda s: (s, 0, 0)),
            pl.BlockSpec((APPLY, points), lambda s: (s, 0)),
        ],
        out_specs=pl.BlockSpec((APPLY, members, points), lambda s: (s, 0, 0)),
        compiler_params=pltpu.CompilerParams(vmem_limit_bytes=32 << 20),
        name="apply",
    )(obs_clusters, transforms, state_pert, state_mean)


def solution(mesh):
    placed = (
        P("region", None, "obs"),
        P("region", "obs"),
        P(("region", "obs"), None, None),
        P(("region", "obs"), None),
        P(("region", "obs"), None),
        P(("region", "obs")),
        P(),
        P("region", "obs"),
        P("region", "obs"),
        P(),
    )
    return jax.shard_map(
        local, mesh=mesh, in_specs=placed, out_specs=P("region", None, "obs"), check_vma=False
    )
```

time: 515 us -> 96.8 us (0.19)
  waiting for transfers between devices: 308 us -> 0 us
  Pallas kernels: 0 us -> 91.3 us
  local copies, waits for them, and re-layouts: 72.9 us -> 4.16 us
  matrix products: 60.2 us -> 0 us
  starting transfers between devices: 28.8 us -> 0 us
  other arithmetic: 15.2 us -> 0.83 us
  between operations: 14.3 us -> 0.04 us
  blocking collectives: 13.4 us -> 0 us
    all_to_all x3 -> x0, waiting for transfers between devices: 286 us -> none  [the longest x1 183 us: local(): lax.all_to_all(into_slots(gram_sums), 'region', split_axis=0, concat_axis...]
    pallas_call x0 -> x2, Pallas kernels: none -> 91.3 us  [the longest x1 83 us: local(): pl.pallas_call(solve_kernel, out_shape=jax.ShapeDtypeStruct((clusters, me...]
    dot_general x41 -> x0, matrix products: 60.2 us -> none  [the longest x37 35 us: product(): jnp.einsum('cij,cjk->cik', left, right, precision=lax.Precision.HIGHEST)]
    scatter x4 -> x0, local copies, waits for them, and re-layouts: 40.2 us -> none  [the longest x2 25 us: into_slots(): return jnp.zeros((slot_total,) + values.shape[1:], values.dtype).at[slot_...]
    all_to_all x3 -> x0, starting transfers between devices: 28.7 us -> none  [the longest x1 11.9 us: local(): lax.all_to_all(back, 'region', split_axis=0, concat_axis=0, tiled=True)]
    gather x7 -> x0, local copies, waits for them, and re-layouts: 22.4 us -> none  [the longest x1 8.6 us: local(): cluster_pert = obs_pert[block_list]]
    all_gather x1 -> x0, waiting for transfers between devices: 22.3 us -> none  [local(): all_transforms = lax.all_gather(my_transforms, 'obs', axis=0, tiled=True)]
    unnamed x1 -> x0, blocking collectives: 13.4 us -> none
  transfers between devices with their start and end apart: 5 -> 0, of which waited for: 4 -> 0; matrix products, arithmetic and copies ran while one was open for 3% -> 0% of each run, Pallas kernels for 0% -> 0%
where the time goes in v1:
time: 96.8 us; the launch traced here: 96.3 us
  Pallas kernels  91.3 us (94%)
  local copies, waits for them, and re-layouts  4.16 us (4%)
    pallas_call x1, Pallas kernels, local(): pl.pallas_call(solve_kernel, out_shape=jax.ShapeDtypeStruct((clusters, me...  83 us
    pallas_call x1, Pallas kernels, local(): pl.pallas_call(apply_kernel, grid=(clusters // APPLY,), out_shape=jax.Sha...  8.27 us
    unnamed x16, local copies, waits for them, and re-layouts  4.16 us

profile of v1, /device:TPU:1, one launch (start us, length us, event | category | flops | bytes accessed | tf_op | source)
XLA Modules:
  0.0 96.3 jit_solution(17822605335928151079)
XLA Ops:
  0.0 0.0 copy-start
  0.0 0.8 fusion
  0.8 0.0 copy-start.1
  0.8 1.4 %copy-done.1 = bf16[32,128,128]{2,1,0:T(8,128)(2,1)S(1)} copy-done((bf16[32,128,128]{2,1,0:T(8,128)(2,1)S(1)}, bf16[32,128,128]{2,1,0:T(8,128)(2,1)}, u32[]{:S(2)}) %copy-start.1) | copy-done | bytes 1048600
  2.2 0.0 copy-start.3
  2.3 0.7 copy-done.3
  3.0 0.0 copy-start.4
  3.0 0.7 copy-done.4
  3.7 0.0 copy-start.5
  3.7 0.7 copy-done.5
  4.3 0.0 copy-start.6
  4.3 0.7 copy-done.6
  5.0 0.0 copy-start.2
  5.0 0.0 copy-start.7
  5.0 83.0 %solve.1.t_ref = bf16[128,128,128]{2,1,0:T(8,128)(2,1)S(1)} custom-call(s32[8,128]{1,0:T(8,128)S(1)} %pad.4.lists_ref, s32[32]{0:T(128)S(1)} %copy-done.5, f32[8]{0:T(128)S(1)} %copy-done.6, f32[32,128]{1,0:T(8,128)S(1)} %copy-done.3, f32[32,128]{1,0:T(8,128)S(1)} %copy-done.4, bf16[32,128,128]{2,1,0:T(8,128)(2,1)S(1)} %copy-done.1), custom_call_target="tpu_custom_call" | custom-call | tf_op jit(solution)/shard_map/solve/pallas_call | solution.py:252
  88.0 0.0 copy-done
  88.1 0.0 copy-done.2
  88.1 0.0 copy-done.7
  88.1 8.3 %apply.1 = bf16[128,128,128]{2,1,0:T(8,128)(2,1)} custom-call(s32[64]{0:T(128)S(1)} %copy-done.7, bf16[128,128,128]{2,1,0:T(8,128)(2,1)S(1)} %solve.1.t_ref, bf16[128,128,128]{2,1,0:T(8,128)(2,1)S(1)} %copy-done, f32[128,128]{1,0:T(8,128)S(1)} %copy-done.2), custom_call_target="tpu_custom_call" | custom-call | tf_op jit(solution)/shard_map/apply/pallas_call | solution.py:278
  (1 shorter events, 0.0 us)
Async XLA Ops:
  0.0 88.1 %copy-start = (bf16[128,128,128]{2,1,0:T(8,128)(2,1)S(1)}, bf16[128,128,128]{2,1,0:T(8,128)(2,1)}, u32[]{:S(2)}) copy-start(bf16[128,128,128]{2,1,0:T(8,128)(2,1)} %x_ref.1) | copy-start | bytes 12582916
  0.8 1.4 %copy-start.1 = (bf16[32,128,128]{2,1,0:T(8,128)(2,1)S(1)}, bf16[32,128,128]{2,1,0:T(8,128)(2,1)}, u32[]{:S(2)}) copy-start(bf16[32,128,128]{2,1,0:T(8,128)(2,1)} %pool_ref.1) | copy-start | bytes 3145732
  2.2 0.7 copy-start.3
  3.0 0.7 copy-start.4
  3.7 0.7 copy-start.5
  4.3 0.7 copy-start.6
  5.0 83.1 %copy-start.2 = (f32[128,128]{1,0:T(8,128)S(1)}, f32[128,128]{1,0:T(8,128)}, u32[]{:S(2)}) copy-start(f32[128,128]{1,0:T(8,128)} %mean_ref.1) | copy-start | bytes 196612
  5.0 83.1 %copy-start.7 = (s32[64]{0:T(128)S(1)}, s32[64]{0:T(128)}, u32[]{:S(2)}) copy-start(s32[64]{0:T(128)} %count_ref.1) | copy-start | bytes 772

commit v2 on v1

v2 whole, which is shorter than its diff:
```python
import functools

import jax
import jax.numpy as jnp
from jax import lax
from jax.experimental import pallas as pl
from jax.experimental.pallas import tpu as pltpu
from jax.sharding import PartitionSpec as P

MESH = pl.DeviceIdType.MESH
BF = jnp.bfloat16
F32 = jnp.float32
K = 128
OBS = 4
CORES = 2
POOL = 32
SLOTS = POOL + 1
CHUNKS = 8
PER = POOL // CHUNKS
GROUP = 8
OWN = 32
GROUPS = OWN // GROUP
UNIT = 4
UNITS = GROUP // UNIT
PACKED = UNIT // 2 * K + 16
COEF = (2.25, -2.4375, 1.6875, -0.5625, 0.0625)


def split(a):
    high = a.astype(BF)
    return high, (a - high.astype(F32)).astype(BF)


def product(left, right):
    left_high, left_low = left
    right_high, right_low = right
    row = jnp.concatenate([right_high, right_low], axis=1)
    both = jnp.dot(
        jnp.concatenate([left_high, left_low], axis=1),
        jnp.concatenate([row, row], axis=0),
        preferred_element_type=F32,
    )
    return both[:, :K] + both[:, K:]


def inverse_root(matrices, eye):
    every = range(len(matrices))
    w = list(matrices)
    w_parts = [split(a) for a in w]
    y, z = w_parts, None
    for step in range(6):
        if step:
            w = [product(z[i], y[i]) for i in every]
            w_parts = [split(a) for a in w]
        w2 = [product(a, a) for a in w_parts]
        tail = [split(COEF[3] * w[i] + COEF[4] * w2[i]) for i in every]
        w2_parts = [split(a) for a in w2]
        turn = [
            (COEF[0] * eye + COEF[1] * w[i]) + (COEF[2] * w2[i] + product(w2_parts[i], tail[i]))
            for i in every
        ]
        turn_parts = [split(a) for a in turn]
        if step < 5:
            y = [split(product(y[i], turn_parts[i])) for i in every]
        if step:
            z_full = [product(turn_parts[i], z[i]) for i in every]
            z = [split(a) for a in z_full]
        else:
            z = turn_parts
    return z_full, z


def places():
    rows = lax.broadcasted_iota(jnp.int32, (K, K), 0)
    columns = lax.broadcasted_iota(jnp.int32, (K, K), 1)
    return rows, columns


def solve_kernel(
    list_ref, count_ref, type_ref, prec_ref, weight_ref, innov_ref, pool_ref, out_ref,
    in_list, in_count, in_type, in_prec, in_weight, in_innov,
    pool, own_rows, own_lists, rows, lists, index, gram, proj, mine,
    in_sem, local_sem, small_send, small_recv, send, twin_send, recv,
    t_local, t_send, t_recv, f_send, f_recv,
):
    me, region = lax.axis_index("obs"), lax.axis_index("region")
    core = lax.rem(region, CORES)
    base = region - core
    twin = base + 1 - core
    partner, cross, far = me + 1 - 2 * lax.rem(me, 2), 3 - me, lax.rem(me + 2, OBS)
    tile = me // 2
    primary = core == tile
    solver = lax.rem(me, 2) * CORES + core

    def remote(src, dst, send_sem, recv_sem, to_region, to):
        return pltpu.make_async_remote_copy(
            src_ref=src, dst_ref=dst, send_sem=send_sem, recv_sem=recv_sem,
            device_id={"region": to_region, "obs": to}, device_id_type=MESH,
        )

    barrier = pltpu.get_barrier_semaphore()
    for other in range(1, OBS):
        for c in range(CORES):
            pl.semaphore_signal(
                barrier, inc=1, device_id={"region": base + c, "obs": lax.rem(me + other, OBS)}, device_id_type=MESH
            )
    pl.semaphore_signal(barrier, inc=1, device_id={"region": twin, "obs": me}, device_id_type=MESH)

    reads = []
    for j, (src, dst) in enumerate((
        (type_ref, in_type), (prec_ref, in_prec), (weight_ref, in_weight),
        (innov_ref, in_innov), (list_ref, in_list), (count_ref, in_count),
    )):
        reads.append(pltpu.make_async_copy(src, dst, in_sem.at[j]))
        reads[-1].start()
    for c in reads:
        c.wait()

    @pl.when(primary)
    def _():
        pltpu.make_async_copy(pool_ref, pool.at[me], local_sem).start()

    for b in range(POOL):
        weighted = in_weight[pl.ds(b, 1), :] * in_prec[in_type[b]]
        own_rows[pl.ds(b, 1), :] = weighted.astype(BF).astype(F32)
        own_rows[pl.ds(POOL + b, 1), :] = (weighted * in_innov[pl.ds(b, 1), :]).astype(BF).astype(F32)
    entry = lax.broadcasted_iota(jnp.int32, (2, K), 0)
    own_lists[...] = jnp.full((8, K), POOL, jnp.int32)
    own_lists[pl.ds(0, 2), :] = jnp.where(entry < in_count[...], in_list[...], POOL)
    place_row, place_column = places()
    eye = (place_row == place_column).astype(F32)
    for o in range(OBS):
        gram[o * SLOTS + POOL] = jnp.zeros((K, K), F32)
        proj[o, pl.ds(POOL, 8), :] = jnp.zeros((8, K), F32)
    pl.semaphore_wait(barrier, 7)

    def small(j, a, c):
        src, dst = ((own_rows, rows), (own_lists, lists))[j]
        return remote(src, dst.at[me], small_send.at[j, a, c], small_recv.at[j, me], base + c, 2 * core + a)

    def elsewhere(a, c):
        return jnp.logical_not(jnp.logical_and(primary, jnp.logical_and(2 * core + a == me, core == c)))

    for a in range(2):
        for c in range(CORES):
            @pl.when(elsewhere(a, c))
            def _():
                for j in range(2):
                    small(j, a, c).start()

    def piece(o, k):
        return pool.at[o, pl.ds(k * PER, PER)]

    def to_chip(src, o, k, to):
        return remote(src, piece(o, k), send.at[o, k], recv.at[o, k], region, to)

    def to_twin(src, o, k):
        return remote(src, piece(o, k), twin_send.at[o, k], recv.at[o, k], twin, me)

    def own_piece(k):
        return pool_ref.at[pl.ds(k * PER, PER)]

    @pl.when(primary)
    def _():
        def body(k, _):
            to_chip(own_piece(k), me, k, partner).start()
            to_twin(own_piece(k), me, k).start()
            return 0

        lax.fori_loop(0, CHUNKS, body, 0)
        rows[me] = own_rows[...]
        lists[me] = own_lists[...]

    @pl.when(jnp.logical_not(primary))
    def _():
        def body(k, _):
            to_chip(own_piece(k), me, k, cross).start()
            return 0

        lax.fori_loop(0, CHUNKS, body, 0)

    def arrived(o, k):
        to_twin(piece(o, k), o, k).wait_recv()

    def block_grams(o, k):
        for j in range(PER):
            b = k * PER + j
            pert = pool[o, b]
            weight = rows[o, pl.ds(b, 1), :]
            innov = rows[o, pl.ds(POOL + b, 1), :]
            scaled = (pert.astype(F32) * weight).astype(BF)
            lhs = jnp.concatenate([scaled, jnp.broadcast_to(innov, (16, K)).astype(BF)], axis=0)
            res = lax.dot_general(lhs, pert, (((1,), (1,)), ((), ())), preferred_element_type=F32)
            gram[o * SLOTS + b] = res[:K]
            proj[o, pl.ds(b, 1), :] = res[K:K + 1]

    def hand_on(k):
        @pl.when(k < CHUNKS)
        def _():
            arrived(cross, k)

            @pl.when(primary)
            def _():
                to_chip(piece(cross, k), cross, k, partner).start()
                to_twin(piece(cross, k), cross, k).start()

            arrived(partner, k)

            @pl.when(primary)
            def _():
                to_twin(piece(partner, k), partner, k).start()

        @pl.when(k >= 2)
        def _():
            arrived(far, k - 2)

            @pl.when(primary)
            def _():
                to_twin(piece(far, k - 2), far, k - 2).start()

    hand_on(0)
    hand_on(1)
    for o in range(OBS):
        @pl.when(jnp.logical_not(jnp.logical_and(primary, me == o)))
        def _():
            for j, (src, dst) in enumerate(((own_rows, rows), (own_lists, lists))):
                remote(src, dst.at[o], small_send.at[j, 0, 0], small_recv.at[j, o], twin, me).wait_recv()
    to_index = pltpu.make_async_copy(lists, index, in_sem.at[0])
    to_index.start()

    @pl.when(primary)
    def _():
        pltpu.make_async_copy(pool_ref, pool.at[me], local_sem).wait()

    def step(k, _):
        hand_on(k)

        @pl.when(jnp.logical_not(primary))
        def _():
            arrived(me, k - 2)

        for o in (me, cross, partner):
            block_grams(o, k - 2)

        @pl.when(k >= 3)
        def _():
            block_grams(far, k - 3)

        return 0

    lax.fori_loop(2, CHUNKS + 2, step, 0)
    block_grams(far, CHUNKS - 1)
    to_index.wait()

    def slot(of, g, unit, size):
        return out_ref.at[pl.ds(of * (OWN // UNIT) + g * UNITS + unit, size)]

    def unit_of(g, unit, size):
        return mine.at[pl.ds(g * UNITS + unit, size)]

    def t_first(j, of, g, unit, to):
        return remote(
            unit_of(g, unit, 1), slot(of, g, unit, 1), t_send.at[j, g, unit], t_recv.at[of, g, unit], base + tile, to
        )

    def t_keep(g):
        return pltpu.make_async_copy(unit_of(g, 0, UNITS), slot(solver, g, 0, UNITS), t_local.at[g])

    primary_int = primary.astype(jnp.int32)
    heard = primary_int * partner + (1 - primary_int) * cross
    onward = primary_int * cross + (1 - primary_int) * partner
    part = 1 - primary_int

    def t_pass(of, h, g, c, to):
        half = slot(of, g, h, 1)
        return remote(half, half, f_send.at[c, g], f_recv.at[of, h, g], region, to)

    def forward(g):
        for c in range(CORES):
            of = lax.rem(heard, 2) * CORES + c
            t_first(0, of, g, part, heard).wait_recv()
            t_pass(of, part, g, c, onward).start()

    upper = place_column >= place_row

    def solve_group(g, _):
        matrices, norms, vectors = [], [], []
        for i in range(GROUP):
            c = solver * OWN + g * GROUP + i
            total, vector = None, None
            for o in range(OBS):
                for m in range(2):
                    b = index[o, m, c]
                    one, row = gram[o * SLOTS + b], proj[o, pl.ds(b, 1), :]
                    total = one if total is None else total + one
                    vector = row if vector is None else vector + row
            matrix = eye + total * (1.0 / 127.0)
            square = jnp.sum(jnp.sum(matrix * matrix, axis=0, keepdims=True), axis=1, keepdims=True)
            scale = lax.rsqrt(square)
            matrices.append(matrix * scale)
            norms.append(scale)
            vectors.append(vector)
        full, parts = inverse_root(matrices, eye)
        for u in range(UNITS):
            extra = []
            for q in range(UNIT // 2):
                roots, means = [], []
                for i in (u * UNIT + 2 * q, u * UNIT + 2 * q + 1):
                    row = jnp.broadcast_to(vectors[i] * (norms[i] * (1.0 / 127.0)), (16, K))
                    row = product(split(row), parts[i])
                    row = product(split(row), parts[i])[0:1]
                    roots.append(full[i] * jnp.sqrt(norms[i]))
                    means += split(row)
                extra += [jnp.sum(roots[1] * eye, axis=0, keepdims=True).astype(BF)] + means
                mine[g * UNITS + u, pl.ds(q * K, K), :] = jnp.where(upper, roots[0], roots[1]).astype(BF)
            extra.append(jnp.zeros((16 - len(extra), K), BF))
            mine[g * UNITS + u, pl.ds(UNIT // 2 * K, 16), :] = jnp.concatenate(extra, axis=0)
        for j, unit, to in ((0, 0, partner), (1, 1, cross), (0, 1, partner), (1, 0, cross)):
            t_first(j, solver, g, unit, to).start()

        @pl.when(primary)
        def _():
            t_keep(g).start()

        @pl.when(jnp.logical_not(primary))
        def _():
            for unit in range(UNITS):
                t_first(2, solver, g, unit, me).start()

        @pl.when(g > 0)
        def _():
            forward(g - 1)

        return 0

    lax.fori_loop(0, GROUPS, solve_group, 0)
    forward(GROUPS - 1)

    @pl.when(primary)
    def _():
        for g in range(GROUPS):
            for unit in range(UNITS):
                t_first(2, lax.rem(me, 2) * CORES + 1 - core, g, unit, me).wait_recv()
            t_keep(g).wait()

        for k in range(CHUNKS):
            to_chip(own_piece(k), me, k, partner).wait_send()
            to_chip(piece(cross, k), cross, k, partner).wait_send()
            to_twin(own_piece(k), me, k).wait_send()
            for o in (cross, partner, far):
                to_twin(piece(o, k), o, k).wait_send()

    @pl.when(jnp.logical_not(primary))
    def _():
        for g in range(GROUPS):
            for c in range(CORES):
                of = lax.rem(far, 2) * CORES + c
                for h in range(2):
                    t_pass(of, h, g, c, onward).wait_recv()
            for unit in range(UNITS):
                t_first(2, solver, g, unit, me).wait_send()

        for k in range(CHUNKS):
            to_chip(own_piece(k), me, k, cross).wait_send()

    for g in range(GROUPS):
        for unit in range(UNITS):
            t_first(0, solver, g, unit, partner).wait_send()
            t_first(1, solver, g, unit, cross).wait_send()
        for c in range(CORES):
            of = lax.rem(heard, 2) * CORES + c
            t_first(0, of, g, 1 - part, heard).wait_recv()
            t_pass(of, part, g, c, onward).wait_send()
    for a in range(2):
        for c in range(CORES):
            @pl.when(elsewhere(a, c))
            def _():
                for j in range(2):
                    small(j, a, c).wait_send()


APPLY = 16


def apply_kernel(clusters, count_ref, packed_ref, x_ref, mean_ref, out_ref, packed_in, x_in, result, in_sem, out_sem):
    count = count_ref[lax.axis_index("region")]
    steps = clusters // APPLY

    def reads(s):
        here, units = pl.ds(s * APPLY, APPLY), pl.ds(s * (APPLY // UNIT), APPLY // UNIT)
        return (
            pltpu.make_async_copy(packed_ref.at[units], packed_in.at[units], in_sem.at[0, s]),
            pltpu.make_async_copy(x_ref.at[here], x_in.at[here], in_sem.at[1, s]),
        )

    def write(s):
        here = pl.ds(s * APPLY, APPLY)
        return pltpu.make_async_copy(result.at[here], out_ref.at[here], out_sem.at[s])

    for s in range(steps):
        for c in reads(s):
            c.start()
    place_row, place_column = places()
    diagonal, upper, lower = place_row == place_column, place_column >= place_row, place_column < place_row

    def body(s, _):
        for c in reads(s):
            c.wait()
        for u in range(APPLY // UNIT):
            unit = s * (APPLY // UNIT) + u
            extra = packed_in[unit, pl.ds(UNIT // 2 * K, 16), :].astype(F32)
            for q in range(UNIT // 2):
                packed = packed_in[unit, pl.ds(q * K, K), :]
                straight = packed.astype(F32)
                turned = straight.T
                roots = (
                    jnp.where(upper, straight, turned),
                    jnp.where(lower, straight, jnp.where(diagonal, extra[5 * q:5 * q + 1], turned)),
                )
                for i in range(2):
                    c = unit * UNIT + 2 * q + i
                    m = 5 * q + 1 + 2 * i
                    solved = (roots[i] + (extra[m:m + 1] + extra[m + 1:m + 2])).astype(BF)
                    x = x_in[c]
                    mixed = jnp.dot(solved, x, preferred_element_type=F32)
                    mixed = jnp.where(c < count, mixed, x.astype(F32))
                    result[c] = (mixed + mean_ref[pl.ds(c, 1), :]).astype(BF)
        write(s).start()
        return 0

    lax.fori_loop(0, steps, body, 0)
    for s in range(steps):
        write(s).wait()


def local(
    state_pert, state_mean, obs_pert, innov, obs_weight, block_type, type_prec, block_list, block_count, obs_clusters
):
    clusters, members, points = state_pert.shape
    dma = pltpu.SemaphoreType.DMA
    vmem, smem = pl.BlockSpec(memory_space=pltpu.VMEM), pl.BlockSpec(memory_space=pltpu.SMEM)
    hbm, anywhere = pl.BlockSpec(memory_space=pltpu.HBM), pl.BlockSpec(memory_space=pl.ANY)
    packed = pl.pallas_call(
        solve_kernel,
        out_shape=jax.ShapeDtypeStruct((clusters // UNIT, PACKED, members), BF),
        in_specs=[hbm] * 7,
        out_specs=anywhere,
        scratch_shapes=[
            pltpu.VMEM((2, clusters), jnp.int32),
            pltpu.VMEM((1, clusters), jnp.int32),
            pltpu.SMEM((POOL,), jnp.int32),
            pltpu.SMEM(type_prec.shape, F32),
            pltpu.VMEM((POOL, K), F32),
            pltpu.VMEM((POOL, K), F32),
            pltpu.VMEM((OBS, POOL, members, K), BF),
            pltpu.VMEM((2 * POOL, K), F32),
            pltpu.VMEM((8, clusters), jnp.int32),
            pltpu.VMEM((OBS, 2 * POOL, K), F32),
            pltpu.VMEM((OBS, 8, clusters), jnp.int32),
            pltpu.SMEM((OBS, 8, clusters), jnp.int32),
            pltpu.VMEM((OBS * SLOTS, members, members), F32),
            pltpu.VMEM((OBS, POOL + 8, members), F32),
            pltpu.VMEM((OWN // UNIT, PACKED, members), BF),
            dma((6,)), dma,
            dma((2, 2, CORES)), dma((2, OBS)),
            dma((OBS, CHUNKS)), dma((OBS, CHUNKS)), dma((OBS, CHUNKS)),
            dma((GROUPS,)),
            dma((3, GROUPS, UNITS)), dma((OBS, GROUPS, UNITS)),
            dma((CORES, GROUPS)), dma((OBS, 2, GROUPS)),
        ],
        compiler_params=pltpu.CompilerParams(
            collective_id=0, has_side_effects=True, vmem_limit_bytes=60 << 20
        ),
        name="solve",
    )(block_list.T, block_count.T, block_type, type_prec, obs_weight, innov, obs_pert)
    return pl.pallas_call(
        functools.partial(apply_kernel, clusters),
        out_shape=jax.ShapeDtypeStruct(state_pert.shape, BF),
        in_specs=[smem, hbm, hbm, vmem],
        out_specs=hbm,
        scratch_shapes=[
            pltpu.VMEM(packed.shape, BF), pltpu.VMEM(state_pert.shape, BF), pltpu.VMEM(state_pert.shape, BF),
            dma((2, clusters // APPLY)), dma((clusters // APPLY,)),
        ],
        compiler_params=pltpu.CompilerParams(vmem_limit_bytes=58 << 20),
        name="apply",
    )(obs_clusters, packed, state_pert, state_mean)


def solution(mesh):
    placed = (
        P("region", None, "obs"),
        P("region", "obs"),
        P(("region", "obs"), None, None),
        P(("region", "obs"), None),
        P(("region", "obs"), None),
        P(("region", "obs")),
        P(),
        P("region", "obs"),
        P("region", "obs"),
        P(),
    )
    return jax.shard_map(
        local, mesh=mesh, in_specs=placed, out_specs=P("region", None, "obs"), check_vma=False
    )
```

time: 96.8 us -> 70.9 us (0.73)
  Pallas kernels: 91.3 us -> 70.7 us
  local copies, waits for them, and re-layouts: 4.16 us -> 0 us
    pallas_call x2, Pallas kernels: 91.3 us -> 70.7 us  [the longest x1 64.6 us: local(): pl.pallas_call(solve_kernel, out_shape=jax.ShapeDtypeStruct((clusters //...]
    unnamed x16 -> x0, local copies, waits for them, and re-layouts: 4.16 us -> none
where the time goes in v2:
time: 70.9 us; the launch traced here: 70.7 us
  Pallas kernels  70.7 us (100%)
    pallas_call x1, Pallas kernels, local(): pl.pallas_call(solve_kernel, out_shape=jax.ShapeDtypeStruct((clusters //...  64.6 us
    pallas_call x1, Pallas kernels, local(): pl.pallas_call(functools.partial(apply_kernel, clusters), out_shape=jax.S...  6.15 us

profile of v2, /device:TPU:1, one launch (start us, length us, event | category | flops | bytes accessed | tf_op | source)
XLA Modules:
  0.0 70.7 jit_solution(5530330298925785311)
XLA Ops:
  0.0 64.6 %solve.1.packed_ref = bf16[32,272,128]{2,1,0:T(8,128)(2,1)} custom-call(s32[2,128]{1,0:T(2,128)} %bitcast.2, s32[1,128]{1,0:T(1,128)} %bitcast.3, s32[32]{0:T(128)} %type_ref.1, f32[8]{0:T(128)} %prec_ref.1, f32[32,128]{1,0:T(8,128)} %weight_ref.1, f32[32,128]{1,0:T(8,128)} %innov_ref.1, bf16[32,128,128]{2,1,0:T(8,128)(2,1)} %pool_ref.1), custom_call_target="tpu_custom_call" | custom-call | tf_op jit(solution)/shard_map/solve/pallas_call | solution.py:443
  64.6 6.2 %apply.1 = bf16[128,128,128]{2,1,0:T(8,128)(2,1)} custom-call(s32[64]{0:T(128)} %count_ref.1, bf16[32,272,128]{2,1,0:T(8,128)(2,1)} %solve.1.packed_ref, bf16[128,128,128]{2,1,0:T(8,128)(2,1)} %x_ref.1, f32[128,128]{1,0:T(8,128)} %mean_ref.1), custom_call_target="tpu_custom_call" | custom-call | tf_op jit(solution)/shard_map/apply/pallas_call | solution.py:476

commit v3 on v2

--- a/solution.py
+++ b/solution.py
@@ -15,15 +15,16 @@
 CORES = 2
 POOL = 32
 SLOTS = POOL + 1
-CHUNKS = 8
+CHUNKS = 4
 PER = POOL // CHUNKS
+RELAYED = 1
+DIRECT = CHUNKS - RELAYED
 GROUP = 8
 OWN = 32
 GROUPS = OWN // GROUP
 UNIT = 4
 UNITS = GROUP // UNIT
 PACKED = UNIT // 2 * K + 16
-COEF = (2.25, -2.4375, 1.6875, -0.5625, 0.0625)
 
 
 def split(a):
@@ -52,12 +53,9 @@
         if step:
             w = [product(z[i], y[i]) for i in every]
             w_parts = [split(a) for a in w]
-        w2 = [product(a, a) for a in w_parts]
-        tail = [split(COEF[3] * w[i] + COEF[4] * w2[i]) for i in every]
-        w2_parts = [split(a) for a in w2]
+        inner = [split((product(w_parts[i], w_parts[i]) - 4.5 * w[i]) + 3.375 * eye) for i in every]
         turn = [
-            (COEF[0] * eye + COEF[1] * w[i]) + (COEF[2] * w2[i] + product(w2_parts[i], tail[i]))
-            for i in every
+            (1 / 16) * product(inner[i], inner[i]) + ((24.609375 / 16) * eye - (8.625 / 16) * w[i]) for i in every
         ]
         turn_parts = [split(a) for a in turn]
         if step < 5:
@@ -67,7 +65,7 @@
             z = [split(a) for a in z_full]
         else:
             z = turn_parts
-    return z_full, z
+    return z_full
 
 
 def places():
@@ -79,32 +77,44 @@
 def solve_kernel(
     list_ref, count_ref, type_ref, prec_ref, weight_ref, innov_ref, pool_ref, out_ref,
     in_list, in_count, in_type, in_prec, in_weight, in_innov,
-    pool, own_rows, own_lists, rows, lists, index, gram, proj, mine,
-    in_sem, local_sem, small_send, small_recv, send, twin_send, recv,
+    pool, own_rows, own_lists, rows, lists, index, gram, proj, mine, stop,
+    in_sem, local_sem, small_send, small_recv, send, twin_send, recv, r_send, r_recv,
     t_local, t_send, t_recv, f_send, f_recv,
 ):
-    me, region = lax.axis_index("obs"), lax.axis_index("region")
+    at, region = lax.axis_index("obs"), lax.axis_index("region")
     core = lax.rem(region, CORES)
     base = region - core
     twin = base + 1 - core
+    odd = lax.rem(region // CORES, 2)
+    beside = region + CORES * (1 - 2 * odd)
+    me = lax.rem(at + odd, OBS)
     partner, cross, far = me + 1 - 2 * lax.rem(me, 2), 3 - me, lax.rem(me + 2, OBS)
     tile = me // 2
     primary = core == tile
     solver = lax.rem(me, 2) * CORES + core
 
+    me_beside = lax.rem(at + 1 - odd, OBS)
+    relay = core == me_beside // 2
+    partner_beside = me_beside + 1 - 2 * lax.rem(me_beside, 2)
+
+    def place(number):
+        return lax.rem(number - odd + OBS, OBS)
+
     def remote(src, dst, send_sem, recv_sem, to_region, to):
         return pltpu.make_async_remote_copy(
             src_ref=src, dst_ref=dst, send_sem=send_sem, recv_sem=recv_sem,
-            device_id={"region": to_region, "obs": to}, device_id_type=MESH,
+            device_id={"region": to_region, "obs": place(to)}, device_id_type=MESH,
         )
 
     barrier = pltpu.get_barrier_semaphore()
     for other in range(1, OBS):
         for c in range(CORES):
             pl.semaphore_signal(
-                barrier, inc=1, device_id={"region": base + c, "obs": lax.rem(me + other, OBS)}, device_id_type=MESH
+                barrier, inc=1, device_id={"region": base + c, "obs": lax.rem(at + other, OBS)}, device_id_type=MESH
             )
-    pl.semaphore_signal(barrier, inc=1, device_id={"region": twin, "obs": me}, device_id_type=MESH)
+    pl.semaphore_signal(barrier, inc=1, device_id={"region": twin, "obs": at}, device_id_type=MESH)
+    for to in (me, partner, cross):
+        pl.semaphore_signal(barrier, inc=1, device_id={"region": beside, "obs": place(to)}, device_id_type=MESH)
 
     reads = []
     for j, (src, dst) in enumerate((
@@ -132,7 +142,7 @@
     for o in range(OBS):
         gram[o * SLOTS + POOL] = jnp.zeros((K, K), F32)
         proj[o, pl.ds(POOL, 8), :] = jnp.zeros((8, K), F32)
-    pl.semaphore_wait(barrier, 7)
+    pl.semaphore_wait(barrier, 10)
 
     def small(j, a, c):
         src, dst = ((own_rows, rows), (own_lists, lists))[j]
@@ -160,10 +170,23 @@
     def own_piece(k):
         return pool_ref.at[pl.ds(k * PER, PER)]
 
+    def relay_out(k):
+        return remote(own_piece(DIRECT + k), stop.at[k], r_send.at[0, k], r_recv.at[k], beside, partner)
+
+    def relay_back(k):
+        block = piece(partner_beside, DIRECT + k)
+        return remote(stop.at[k], block, r_send.at[1, k], recv.at[partner_beside, DIRECT + k], beside, me)
+
     @pl.when(primary)
     def _():
+        for k in range(RELAYED):
+            relay_out(k).start()
+
         def body(k, _):
-            to_chip(own_piece(k), me, k, partner).start()
+            @pl.when(k < DIRECT)
+            def _():
+                to_chip(own_piece(k), me, k, partner).start()
+
             to_twin(own_piece(k), me, k).start()
             return 0
 
@@ -195,6 +218,11 @@
             proj[o, pl.ds(b, 1), :] = res[K:K + 1]
 
     def hand_on(k):
+        @pl.when(jnp.logical_and(relay, jnp.logical_and(k >= 1, k <= RELAYED)))
+        def _():
+            relay_out(k - 1).wait_recv()
+            relay_back(k - 1).start()
+
         @pl.when(k < CHUNKS)
         def _():
             arrived(cross, k)
@@ -232,23 +260,30 @@
     def _():
         pltpu.make_async_copy(pool_ref, pool.at[me], local_sem).wait()
 
+    def grams(k):
+        @pl.when(jnp.logical_not(primary))
+        def _():
+            arrived(me, k - 2)
+
+        for o in (me, cross, partner):
+            block_grams(o, k - 2)
+
+        @pl.when(k >= 3)
+        def _():
+            block_grams(far, k - 3)
+
     def step(k, _):
         hand_on(k)
-
-        @pl.when(jnp.logical_not(primary))
-        def _():
-            arrived(me, k - 2)
-
-        for o in (me, cross, partner):
-            block_grams(o, k - 2)
-
-        @pl.when(k >= 3)
-        def _():
-            block_grams(far, k - 3)
-
+        grams(k)
         return 0
 
-    lax.fori_loop(2, CHUNKS + 2, step, 0)
+    def last_step(k, _):
+        grams(k)
+        hand_on(k)
+        return 0
+
+    lax.fori_loop(2, CHUNKS, step, 0)
+    lax.fori_loop(CHUNKS, CHUNKS + 2, last_step, 0)
     block_grams(far, CHUNKS - 1)
     to_index.wait()
 
@@ -300,15 +335,15 @@
             matrices.append(matrix * scale)
             norms.append(scale)
             vectors.append(vector)
-        full, parts = inverse_root(matrices, eye)
+        full = inverse_root(matrices, eye)
         for u in range(UNITS):
             extra = []
             for q in range(UNIT // 2):
                 roots, means = [], []
                 for i in (u * UNIT + 2 * q, u * UNIT + 2 * q + 1):
-                    row = jnp.broadcast_to(vectors[i] * (norms[i] * (1.0 / 127.0)), (16, K))
-                    row = product(split(row), parts[i])
-                    row = product(split(row), parts[i])[0:1]
+                    row = vectors[i] * (norms[i] * (1.0 / 127.0))
+                    column = jnp.sum(full[i] * row, axis=1, keepdims=True)
+                    row = jnp.sum(full[i] * column, axis=0, keepdims=True)
                     roots.append(full[i] * jnp.sqrt(norms[i]))
                     means += split(row)
                 extra += [jnp.sum(roots[1] * eye, axis=0, keepdims=True).astype(BF)] + means
@@ -343,8 +378,11 @@
                 t_first(2, lax.rem(me, 2) * CORES + 1 - core, g, unit, me).wait_recv()
             t_keep(g).wait()
 
+        for k in range(DIRECT):
+            to_chip(own_piece(k), me, k, partner).wait_send()
+        for k in range(RELAYED):
+            relay_out(k).wait_send()
         for k in range(CHUNKS):
-            to_chip(own_piece(k), me, k, partner).wait_send()
             to_chip(piece(cross, k), cross, k, partner).wait_send()
             to_twin(own_piece(k), me, k).wait_send()
             for o in (cross, partner, far):
@@ -371,6 +409,11 @@
             of = lax.rem(heard, 2) * CORES + c
             t_first(0, of, g, 1 - part, heard).wait_recv()
             t_pass(of, part, g, c, onward).wait_send()
+    @pl.when(relay)
+    def _():
+        for k in range(RELAYED):
+            relay_back(k).wait_send()
+
     for a in range(2):
         for c in range(CORES):
             @pl.when(elsewhere(a, c))
@@ -382,8 +425,7 @@
 APPLY = 16
 
 
-def apply_kernel(clusters, count_ref, packed_ref, x_ref, mean_ref, out_ref, packed_in, x_in, result, in_sem, out_sem):
-    count = count_ref[lax.axis_index("region")]
+def apply_kernel(clusters, count_ref, packed_ref, x_ref, mean_ref, out_ref, counts, packed_in, x_in, mean, result, in_sem, out_sem):
     steps = clusters // APPLY
 
     def reads(s):
@@ -397,11 +439,22 @@
         here = pl.ds(s * APPLY, APPLY)
         return pltpu.make_async_copy(result.at[here], out_ref.at[here], out_sem.at[s])
 
-    for s in range(steps):
+    small = (
+        pltpu.make_async_copy(count_ref, counts, in_sem.at[0, steps]),
+        pltpu.make_async_copy(mean_ref, mean, in_sem.at[1, steps]),
+    )
+    for c in reads(0) + small:
+        c.start()
+    for s in range(1, steps):
         for c in reads(s):
             c.start()
     place_row, place_column = places()
     diagonal, upper, lower = place_row == place_column, place_column >= place_row, place_column < place_row
+
+    eye = diagonal.astype(BF)
+    for c in small:
+        c.wait()
+    count = counts[lax.axis_index("region")]
 
     def body(s, _):
         for c in reads(s):
@@ -421,10 +474,9 @@
                     c = unit * UNIT + 2 * q + i
                     m = 5 * q + 1 + 2 * i
                     solved = (roots[i] + (extra[m:m + 1] + extra[m + 1:m + 2])).astype(BF)
-                    x = x_in[c]
-                    mixed = jnp.dot(solved, x, preferred_element_type=F32)
-                    mixed = jnp.where(c < count, mixed, x.astype(F32))
-                    result[c] = (mixed + mean_ref[pl.ds(c, 1), :]).astype(BF)
+                    solved = jnp.where(c < count, solved, eye)
+                    mixed = jnp.dot(solved, x_in[c], preferred_element_type=F32)
+                    result[c] = (mixed + mean[pl.ds(c, 1), :]).astype(BF)
         write(s).start()
         return 0
 
@@ -438,7 +490,6 @@
 ):
     clusters, members, points = state_pert.shape
     dma = pltpu.SemaphoreType.DMA
-    vmem, smem = pl.BlockSpec(memory_space=pltpu.VMEM), pl.BlockSpec(memory_space=pltpu.SMEM)
     hbm, anywhere = pl.BlockSpec(memory_space=pltpu.HBM), pl.BlockSpec(memory_space=pl.ANY)
     packed = pl.pallas_call(
         solve_kernel,
@@ -461,9 +512,11 @@
             pltpu.VMEM((OBS * SLOTS, members, members), F32),
             pltpu.VMEM((OBS, POOL + 8, members), F32),
             pltpu.VMEM((OWN // UNIT, PACKED, members), BF),
+            pltpu.VMEM((RELAYED, PER, members, K), BF),
             dma((6,)), dma,
             dma((2, 2, CORES)), dma((2, OBS)),
             dma((OBS, CHUNKS)), dma((OBS, CHUNKS)), dma((OBS, CHUNKS)),
+            dma((2, RELAYED)), dma((RELAYED,)),
             dma((GROUPS,)),
             dma((3, GROUPS, UNITS)), dma((OBS, GROUPS, UNITS)),
             dma((CORES, GROUPS)), dma((OBS, 2, GROUPS)),
@@ -476,11 +529,13 @@
     return pl.pallas_call(
         functools.partial(apply_kernel, clusters),
         out_shape=jax.ShapeDtypeStruct(state_pert.shape, BF),
-        in_specs=[smem, hbm, hbm, vmem],
+        in_specs=[hbm] * 4,
         out_specs=hbm,
         scratch_shapes=[
-            pltpu.VMEM(packed.shape, BF), pltpu.VMEM(state_pert.shape, BF), pltpu.VMEM(state_pert.shape, BF),
-            dma((2, clusters // APPLY)), dma((clusters // APPLY,)),
+            pltpu.SMEM(obs_clusters.shape, jnp.int32),
+            pltpu.VMEM(packed.shape, BF), pltpu.VMEM(state_pert.shape, BF),
+            pltpu.VMEM(state_mean.shape, F32), pltpu.VMEM(state_pert.shape, BF),
+            dma((2, clusters // APPLY + 1)), dma((clusters // APPLY,)),
         ],
         compiler_params=pltpu.CompilerParams(vmem_limit_bytes=58 << 20),
         name="apply",

time: 70.9 us -> 65.8 us (0.928)
  Pallas kernels: 70.7 us -> 65.7 us
    pallas_call x1, Pallas kernels: 64.6 us -> 60.4 us  [local(): pl.pallas_call(solve_kernel, out_shape=jax.ShapeDtypeStruct((clusters //...]
    pallas_call x1, Pallas kernels: 6.15 us -> 5.35 us  [local(): pl.pallas_call(functools.partial(apply_kernel, clusters), out_shape=jax.S...]
where the time goes in v3:
time: 65.8 us; the launch traced here: 65.7 us
  Pallas kernels  65.7 us (100%)
    pallas_call x1, Pallas kernels, local(): pl.pallas_call(solve_kernel, out_shape=jax.ShapeDtypeStruct((clusters //...  60.4 us
    pallas_call x1, Pallas kernels, local(): pl.pallas_call(functools.partial(apply_kernel, clusters), out_shape=jax.S...  5.35 us

profile of v3, /device:TPU:1, one launch (start us, length us, event | category | flops | bytes accessed | tf_op | source)
XLA Modules:
  0.0 65.7 jit_solution(10045048398389274560)
XLA Ops:
  0.0 60.4 %solve.1.packed_ref = bf16[32,272,128]{2,1,0:T(8,128)(2,1)} custom-call(s32[2,128]{1,0:T(2,128)} %bitcast.2, s32[1,128]{1,0:T(1,128)} %bitcast.3, s32[32]{0:T(128)} %type_ref.1, f32[8]{0:T(128)} %prec_ref.1, f32[32,128]{1,0:T(8,128)} %weight_ref.1, f32[32,128]{1,0:T(8,128)} %innov_ref.1, bf16[32,128,128]{2,1,0:T(8,128)(2,1)} %pool_ref.1), custom_call_target="tpu_custom_call" | custom-call | tf_op jit(solution)/shard_map/solve/pallas_call | solution.py:494
  60.4 5.3 %apply.1 = bf16[128,128,128]{2,1,0:T(8,128)(2,1)} custom-call(s32[64]{0:T(128)} %count_ref.1, bf16[32,272,128]{2,1,0:T(8,128)(2,1)} %solve.1.packed_ref, bf16[128,128,128]{2,1,0:T(8,128)(2,1)} %x_ref.1, f32[128,128]{1,0:T(8,128)} %mean_ref.1), custom_call_target="tpu_custom_call" | custom-call | tf_op jit(solution)/shard_map/apply/pallas_call | solution.py:529

commit v4 on v3

--- a/solution.py
+++ b/solution.py
@@ -44,28 +44,39 @@
     return both[:, :K] + both[:, K:]
 
 
-def inverse_root(matrices, eye):
-    every = range(len(matrices))
-    w = list(matrices)
-    w_parts = [split(a) for a in w]
+def root_stages(matrix, eye, result):
+    w, w_parts = matrix, split(matrix)
     y, z = w_parts, None
     for step in range(6):
         if step:
-            w = [product(z[i], y[i]) for i in every]
-            w_parts = [split(a) for a in w]
-        inner = [split((product(w_parts[i], w_parts[i]) - 4.5 * w[i]) + 3.375 * eye) for i in every]
-        turn = [
-            (1 / 16) * product(inner[i], inner[i]) + ((24.609375 / 16) * eye - (8.625 / 16) * w[i]) for i in every
-        ]
-        turn_parts = [split(a) for a in turn]
+            w = product(z, y)
+            yield
+            w_parts = split(w)
+        inner = (product(w_parts, w_parts) - 4.5 * w) + 3.375 * eye
+        yield
+        inner = split(inner)
+        turn = (1 / 16) * product(inner, inner) + ((24.609375 / 16) * eye - (8.625 / 16) * w)
+        yield
+        turn = split(turn)
         if step < 5:
-            y = [split(product(y[i], turn_parts[i])) for i in every]
+            y = split(product(y, turn))
         if step:
-            z_full = [product(turn_parts[i], z[i]) for i in every]
-            z = [split(a) for a in z_full]
+            full = product(turn, z)
+            z = split(full)
         else:
-            z = turn_parts
-    return z_full
+            z = turn
+        yield
+    result.append(full)
+
+
+def inverse_root(matrices, eye):
+    results = [[] for _ in matrices]
+    live = [root_stages(matrix, eye, result) for matrix, result in zip(matrices, results)]
+    for ahead in live[::2]:
+        next(ahead)
+    while live:
+        live = [stages for stages in live if next(stages, True) is None]
+    return [result[0] for result in results]
 
 
 def places():
@@ -422,7 +433,7 @@
                     small(j, a, c).wait_send()
 
 
-APPLY = 16
+APPLY = 32
 
 
 def apply_kernel(clusters, count_ref, packed_ref, x_ref, mean_ref, out_ref, counts, packed_in, x_in, mean, result, in_sem, out_sem):

time: 65.8 us -> 64.1 us (0.974)
  Pallas kernels: 65.7 us -> 64 us
    pallas_call x1, Pallas kernels: 60.4 us -> 58.9 us  [local(): pl.pallas_call(solve_kernel, out_shape=jax.ShapeDtypeStruct((clusters //...]
where the time goes in v4:
time: 64.1 us; the launch traced here: 64 us
  Pallas kernels  64 us (100%)
    pallas_call x1, Pallas kernels, local(): pl.pallas_call(solve_kernel, out_shape=jax.ShapeDtypeStruct((clusters //...  58.9 us
    pallas_call x1, Pallas kernels, local(): pl.pallas_call(functools.partial(apply_kernel, clusters), out_shape=jax.S...  5.08 us

profile of v4, /device:TPU:1, one launch (start us, length us, event | category | flops | bytes accessed | tf_op | source)
XLA Modules:
  0.0 64.0 jit_solution(15082247966893545161)
XLA Ops:
  0.0 58.9 %solve.1.packed_ref = bf16[32,272,128]{2,1,0:T(8,128)(2,1)} custom-call(s32[2,128]{1,0:T(2,128)} %bitcast.2, s32[1,128]{1,0:T(1,128)} %bitcast.3, s32[32]{0:T(128)} %type_ref.1, f32[8]{0:T(128)} %prec_ref.1, f32[32,128]{1,0:T(8,128)} %weight_ref.1, f32[32,128]{1,0:T(8,128)} %innov_ref.1, bf16[32,128,128]{2,1,0:T(8,128)(2,1)} %pool_ref.1), custom_call_target="tpu_custom_call" | custom-call | tf_op jit(solution)/shard_map/solve/pallas_call | solution.py:505
  58.9 5.1 %apply.1 = bf16[128,128,128]{2,1,0:T(8,128)(2,1)} custom-call(s32[64]{0:T(128)} %count_ref.1, bf16[32,272,128]{2,1,0:T(8,128)(2,1)} %solve.1.packed_ref, bf16[128,128,128]{2,1,0:T(8,128)(2,1)} %x_ref.1, f32[128,128]{1,0:T(8,128)} %mean_ref.1), custom_call_target="tpu_custom_call" | custom-call | tf_op jit(solution)/shard_map/apply/pallas_call | solution.py:540

commit v5 on v4

--- a/solution.py
+++ b/solution.py
@@ -229,10 +229,12 @@
             proj[o, pl.ds(b, 1), :] = res[K:K + 1]
 
     def hand_on(k):
-        @pl.when(jnp.logical_and(relay, jnp.logical_and(k >= 1, k <= RELAYED)))
-        def _():
-            relay_out(k - 1).wait_recv()
-            relay_back(k - 1).start()
+        first = isinstance(k, int)
+        if not first or 1 <= k <= RELAYED:
+            @pl.when(jnp.logical_and(relay, jnp.logical_and(k >= 1, k <= RELAYED)))
+            def _():
+                relay_out(k - 1).wait_recv()
+                relay_back(k - 1).start()
 
         @pl.when(k < CHUNKS)
         def _():
@@ -248,6 +250,9 @@
             @pl.when(primary)
             def _():
                 to_twin(piece(partner, k), partner, k).start()
+
+        if first:
+            return
 
         @pl.when(k >= 2)
         def _():

time: 64.1 us -> 64.1 us (level)
  no operation moved by 1% of the time
where the time goes in v5:
time: 64.1 us; the launch traced here: 64 us
  Pallas kernels  63.9 us (100%)
    pallas_call x1, Pallas kernels, local(): pl.pallas_call(solve_kernel, out_shape=jax.ShapeDtypeStruct((clusters //...  58.9 us
    pallas_call x1, Pallas kernels, local(): pl.pallas_call(functools.partial(apply_kernel, clusters), out_shape=jax.S...  5.08 us

profile of v5, /device:TPU:1, one launch (start us, length us, event | category | flops | bytes accessed | tf_op | source)
XLA Modules:
  0.0 64.0 jit_solution(15082247966893545161)
XLA Ops:
  0.0 58.9 %solve.1.packed_ref = bf16[32,272,128]{2,1,0:T(8,128)(2,1)} custom-call(s32[2,128]{1,0:T(2,128)} %bitcast.2, s32[1,128]{1,0:T(1,128)} %bitcast.3, s32[32]{0:T(128)} %type_ref.1, f32[8]{0:T(128)} %prec_ref.1, f32[32,128]{1,0:T(8,128)} %weight_ref.1, f32[32,128]{1,0:T(8,128)} %innov_ref.1, bf16[32,128,128]{2,1,0:T(8,128)(2,1)} %pool_ref.1), custom_call_target="tpu_custom_call" | custom-call | tf_op jit(solution)/shard_map/solve/pallas_call | solution.py:510
  58.9 5.1 %apply.1 = bf16[128,128,128]{2,1,0:T(8,128)(2,1)} custom-call(s32[64]{0:T(128)} %count_ref.1, bf16[32,272,128]{2,1,0:T(8,128)(2,1)} %solve.1.packed_ref, bf16[128,128,128]{2,1,0:T(8,128)(2,1)} %x_ref.1, f32[128,128]{1,0:T(8,128)} %mean_ref.1), custom_call_target="tpu_custom_call" | custom-call | tf_op jit(solution)/shard_map/apply/pallas_call | solution.py:545

commit v6 on v5

--- a/solution.py
+++ b/solution.py
@@ -451,9 +451,9 @@
             pltpu.make_async_copy(x_ref.at[here], x_in.at[here], in_sem.at[1, s]),
         )
 
-    def write(s):
-        here = pl.ds(s * APPLY, APPLY)
-        return pltpu.make_async_copy(result.at[here], out_ref.at[here], out_sem.at[s])
+    def write(s, half):
+        here = pl.ds(s * APPLY + half * (APPLY // 2), APPLY // 2)
+        return pltpu.make_async_copy(result.at[here], out_ref.at[here], out_sem.at[half, s])
 
     small = (
         pltpu.make_async_copy(count_ref, counts, in_sem.at[0, steps]),
@@ -493,12 +493,15 @@
                     solved = jnp.where(c < count, solved, eye)
                     mixed = jnp.dot(solved, x_in[c], preferred_element_type=F32)
                     result[c] = (mixed + mean[pl.ds(c, 1), :]).astype(BF)
-        write(s).start()
+            if u == APPLY // UNIT // 2 - 1:
+                write(s, 0).start()
+        write(s, 1).start()
         return 0
 
     lax.fori_loop(0, steps, body, 0)
     for s in range(steps):
-        write(s).wait()
+        write(s, 0).wait()
+        write(s, 1).wait()
 
 
 def local(
@@ -551,7 +554,7 @@
             pltpu.SMEM(obs_clusters.shape, jnp.int32),
             pltpu.VMEM(packed.shape, BF), pltpu.VMEM(state_pert.shape, BF),
             pltpu.VMEM(state_mean.shape, F32), pltpu.VMEM(state_pert.shape, BF),
-            dma((2, clusters // APPLY + 1)), dma((clusters // APPLY,)),
+            dma((2, clusters // APPLY + 1)), dma((2, clusters // APPLY)),
         ],
         compiler_params=pltpu.CompilerParams(vmem_limit_bytes=58 << 20),
         name="apply",

time: 64.1 us -> 64 us (level)
  no operation moved by 1% of the time
where the time goes in v6:
time: 64 us; the launch traced here: 63.8 us
  Pallas kernels  63.8 us (100%)
    pallas_call x1, Pallas kernels, local(): pl.pallas_call(solve_kernel, out_shape=jax.ShapeDtypeStruct((clusters //...  58.9 us
    pallas_call x1, Pallas kernels, local(): pl.pallas_call(functools.partial(apply_kernel, clusters), out_shape=jax.S...  4.97 us

profile of v6, /device:TPU:1, one launch (start us, length us, event | category | flops | bytes accessed | tf_op | source)
XLA Modules:
  0.0 63.8 jit_solution(15451524841185065310)
XLA Ops:
  0.0 58.9 %solve.1.packed_ref = bf16[32,272,128]{2,1,0:T(8,128)(2,1)} custom-call(s32[2,128]{1,0:T(2,128)} %bitcast.2, s32[1,128]{1,0:T(1,128)} %bitcast.3, s32[32]{0:T(128)} %type_ref.1, f32[8]{0:T(128)} %prec_ref.1, f32[32,128]{1,0:T(8,128)} %weight_ref.1, f32[32,128]{1,0:T(8,128)} %innov_ref.1, bf16[32,128,128]{2,1,0:T(8,128)(2,1)} %pool_ref.1), custom_call_target="tpu_custom_call" | custom-call | tf_op jit(solution)/shard_map/solve/pallas_call | solution.py:513
  58.9 5.0 %apply.1 = bf16[128,128,128]{2,1,0:T(8,128)(2,1)} custom-call(s32[64]{0:T(128)} %count_ref.1, bf16[32,272,128]{2,1,0:T(8,128)(2,1)} %solve.1.packed_ref, bf16[128,128,128]{2,1,0:T(8,128)(2,1)} %x_ref.1, f32[128,128]{1,0:T(8,128)} %mean_ref.1), custom_call_target="tpu_custom_call" | custom-call | tf_op jit(solution)/shard_map/apply/pallas_call | solution.py:548

commit v7 on v5

--- a/solution.py
+++ b/solution.py
@@ -190,18 +190,17 @@
 
     @pl.when(primary)
     def _():
+        def body(k, _):
+            @pl.when(k < DIRECT)
+            def _():
+                to_chip(own_piece(k), me, k, partner).start()
+
+            to_twin(own_piece(k), me, k).start()
+            return 0
+
+        lax.fori_loop(0, CHUNKS, body, 0)
         for k in range(RELAYED):
             relay_out(k).start()
-
-        def body(k, _):
-            @pl.when(k < DIRECT)
-            def _():
-                to_chip(own_piece(k), me, k, partner).start()
-
-            to_twin(own_piece(k), me, k).start()
-            return 0
-
-        lax.fori_loop(0, CHUNKS, body, 0)
         rows[me] = own_rows[...]
         lists[me] = own_lists[...]
 

time: 64.1 us -> 64.1 us (level)
  no operation moved by 1% of the time
where the time goes in v7:
time: 64.1 us; the launch traced here: 64 us
  Pallas kernels  64 us (100%)
    pallas_call x1, Pallas kernels, local(): pl.pallas_call(solve_kernel, out_shape=jax.ShapeDtypeStruct((clusters //...  58.9 us
    pallas_call x1, Pallas kernels, local(): pl.pallas_call(functools.partial(apply_kernel, clusters), out_shape=jax.S...  5.08 us

profile of v7, /device:TPU:1, one launch (start us, length us, event | category | flops | bytes accessed | tf_op | source)
XLA Modules:
  0.0 64.0 jit_solution(2593457337432194883)
XLA Ops:
  0.0 58.9 %solve.1.packed_ref = bf16[32,272,128]{2,1,0:T(8,128)(2,1)} custom-call(s32[2,128]{1,0:T(2,128)} %bitcast.2, s32[1,128]{1,0:T(1,128)} %bitcast.3, s32[32]{0:T(128)} %type_ref.1, f32[8]{0:T(128)} %prec_ref.1, f32[32,128]{1,0:T(8,128)} %weight_ref.1, f32[32,128]{1,0:T(8,128)} %innov_ref.1, bf16[32,128,128]{2,1,0:T(8,128)(2,1)} %pool_ref.1), custom_call_target="tpu_custom_call" | custom-call | tf_op jit(solution)/shard_map/solve/pallas_call | solution.py:509
  58.9 5.1 %apply.1 = bf16[128,128,128]{2,1,0:T(8,128)(2,1)} custom-call(s32[64]{0:T(128)} %count_ref.1, bf16[32,272,128]{2,1,0:T(8,128)(2,1)} %solve.1.packed_ref, bf16[128,128,128]{2,1,0:T(8,128)(2,1)} %x_ref.1, f32[128,128]{1,0:T(8,128)} %mean_ref.1), custom_call_target="tpu_custom_call" | custom-call | tf_op jit(solution)/shard_map/apply/pallas_call | solution.py:544
